TPU v7x, 512 devices: a whole 4x8x8 slice. The times are simulated.
512 devices in a mesh: ctx: 128 (over y_lo, x, z), mp: 4 (over y_hi, core).
Axes of the slice: x: 4, y: 8 (y_hi: 2, y_lo: 4; y = y_hi * 4 + y_lo), z: 8, core: 2. Of those that a mesh axis runs over, the one named last changes fastest.
Arguments:
- query_rows: bfloat16 [16384, 2048], P('ctx', 'mp'), may hold values from -51 to 51
- key_rows: bfloat16 [16384, 2048], P('ctx', 'mp'), may hold values from -4 to 4
- value_rows: bfloat16 [16384, 2048], P('ctx', 'mp'), may hold values from -6 to 6
- inputs: bfloat16 [16384, 2048], P('ctx', 'mp'), may hold values from -3 to 3
- out_weight: bfloat16 [2048, 2048], P('mp'), may hold values from -0.125 to 0.125
- kernel: float32 [31, 2048], P(None, 'mp'), may hold values from -1 to 1
- cotangent: bfloat16 [16384, 2048], P('ctx', 'mp'), may hold values from -6 to 6
Outputs:
- output: bfloat16 [16384, 2048], P('ctx', 'mp')
- grad_input: bfloat16 [16384, 2048], P('ctx', 'mp')
- grad_query: bfloat16 [16384, 2048], P('ctx', 'mp')
- grad_key: bfloat16 [16384, 2048], P('ctx', 'mp')
- grad_value: bfloat16 [16384, 2048], P('ctx', 'mp')
All inputs are finite; a program needn't handle non-finite values.
Results may differ from a plain program's by a relative error of at most 0.024.
Values may be sent and summed in bfloat16 or wider, within the bound.
A program may use at most 64 MiB of HBM per device.

v0:
```python
import math
import jax
import jax.numpy as jnp
from jax import lax
from jax.sharding import PartitionSpec as P

HDIM = 128
LOOK = 2


def shifted(block, axis, distance):
    devices = range(lax.axis_size(axis))
    route = [(i - distance, i) for i in devices if i - distance in devices]
    return lax.ppermute(block, axis, route)


def with_halo(block, sides, width):
    for axis, dim in sides:
        count = lax.axis_size(axis)
        forward = [(i, i + 1) for i in range(count - 1)]
        backward = [(target, source) for source, target in forward]
        low = lax.ppermute(
            lax.slice_in_dim(block, block.shape[dim] - width, None, axis=dim), axis, forward
        )
        high = lax.ppermute(lax.slice_in_dim(block, 0, width, axis=dim), axis, backward)
        block = jnp.concatenate([low, block, high], axis=dim)
    return block


def kv_move(kv_pair, offset):
    return shifted(kv_pair, "ctx", offset)


def grad_move(part_pair, offset):
    return shifted(part_pair.astype(jnp.bfloat16), "ctx", offset).astype(part_pair.dtype)


def conv_rim(field_rows, rim_width):
    return with_halo(field_rows, (("ctx", 0),), rim_width)


def relay_window(center, move_step):
    lower_list = []
    upper_list = []
    rising = center
    falling = center
    for offset in range(LOOK):
        rising = move_step(rising, 1)
        falling = move_step(falling, -1)
        lower_list.append(rising)
        upper_list.append(falling)
    return lower_list[::-1] + [center] + upper_list


def per_device(query_rows, key_rows, value_rows, inputs, out_weight, kernel, cotangent):
    frames, local_width = query_rows.shape
    local_heads = local_width // HDIM
    score_scale = 1.0 / math.sqrt(HDIM)
    window_len = (2 * LOOK + 1) * frames
    dev_index = lax.axis_index("ctx")
    dev_count = lax.axis_size("ctx")
    owners = dev_index + jnp.arange(window_len, dtype=jnp.int32) // frames - LOOK
    in_range = (owners >= 0) & (owners < dev_count)
    kv_center = jnp.stack([key_rows, value_rows])
    kv_blocks = relay_window(kv_center, kv_move)
    kv_window = jnp.concatenate(kv_blocks, axis=1)
    key_win = kv_window[0].reshape(window_len, local_heads, HDIM)
    value_win = kv_window[1].reshape(window_len, local_heads, HDIM)
    query_heads = query_rows.reshape(frames, local_heads, HDIM)
    scores = (
        jnp.einsum("qhd,khd->hqk", query_heads, key_win, preferred_element_type=jnp.float32)
        * score_scale
    )
    scores = jnp.where(in_range[None, None, :], scores, -jnp.inf)
    row_max = jnp.max(scores, axis=2)
    log_total = row_max + jnp.log(jnp.sum(jnp.exp(scores - row_max[:, :, None]), axis=2))
    attn_probs = jnp.exp(scores - log_total[:, :, None])
    probs_low = attn_probs.astype(jnp.bfloat16)
    attended = jnp.einsum(
        "hqk,khd->qhd", probs_low, value_win, preferred_element_type=jnp.float32
    ).astype(jnp.bfloat16)
    attended_flat = attended.reshape(frames, local_width)
    partial_out = jnp.dot(attended_flat, out_weight, preferred_element_type=jnp.float32)
    mixed = lax.psum_scatter(
        partial_out.astype(jnp.bfloat16), "mp", scatter_dimension=1, tiled=True
    ).astype(jnp.float32)
    hidden = (inputs.astype(jnp.float32) + mixed).astype(jnp.bfloat16)
    taps = kernel.shape[0]
    half_kernel = taps // 2
    hidden_pad = conv_rim(hidden, half_kernel).astype(jnp.float32)
    conv_out = jnp.zeros((frames, local_width), jnp.float32)
    for tap_index in range(taps):
        conv_out = (
            conv_out + kernel[tap_index][None, :] * hidden_pad[tap_index : tap_index + frames]
        )
    conv_gate = jax.nn.sigmoid(conv_out)
    output = (hidden.astype(jnp.float32) + conv_out * conv_gate).astype(jnp.bfloat16)
    grad_conv = (
        cotangent.astype(jnp.float32) * (conv_gate + conv_out * conv_gate * (1.0 - conv_gate))
    ).astype(jnp.bfloat16)
    grad_pad = conv_rim(grad_conv, half_kernel).astype(jnp.float32)
    grad_hidden = cotangent.astype(jnp.float32)
    for tap_index in range(taps):
        first_row = 2 * half_kernel - tap_index
        grad_hidden = (
            grad_hidden + kernel[tap_index][None, :] * grad_pad[first_row : first_row + frames]
        )
    grad_input = grad_hidden.astype(jnp.bfloat16)
    upstream = jnp.einsum(
        "rn,wn->rw",
        lax.all_gather(grad_input, "mp", axis=1, tiled=True),
        out_weight,
        preferred_element_type=jnp.float32,
    ).astype(jnp.bfloat16)
    up_heads = upstream.reshape(frames, local_heads, HDIM)
    row_delta = jnp.sum(up_heads.astype(jnp.float32) * attended.astype(jnp.float32), axis=2).T
    grad_dots = jnp.einsum("qhd,khd->hqk", up_heads, value_win, preferred_element_type=jnp.float32)
    grad_scores = (attn_probs * (grad_dots - row_delta[:, :, None]) * score_scale).astype(
        jnp.bfloat16
    )
    grad_query = jnp.einsum(
        "hqk,khd->qhd", grad_scores, key_win, preferred_element_type=jnp.float32
    )
    grad_query = grad_query.astype(jnp.bfloat16).reshape(frames, local_width)
    key_parts = jnp.einsum(
        "hqk,qhd->khd", grad_scores, query_heads, preferred_element_type=jnp.float32
    )
    value_parts = jnp.einsum(
        "hqk,qhd->khd", probs_low, up_heads, preferred_element_type=jnp.float32
    )
    part_stack = jnp.stack(
        [key_parts.reshape(window_len, local_width), value_parts.reshape(window_len, local_width)]
    )

    def part_block(position):
        return part_stack[:, position * frames : (position + 1) * frames]

    rising = part_block(2 * LOOK)
    offset = 1
    rising = grad_move(rising, 1) + part_block(LOOK + offset)
    rising = grad_move(rising, 1)
    falling = part_block(0)
    offset = 1
    falling = grad_move(falling, -1) + part_block(LOOK - offset)
    falling = grad_move(falling, -1)
    key_sums = part_block(LOOK) + rising + falling
    grad_key = key_sums[0].astype(jnp.bfloat16)
    grad_value = key_sums[1].astype(jnp.bfloat16)
    return (output, grad_input, grad_query, grad_key, grad_value)


def solution(mesh):
    placed = (
        P("ctx", "mp"),
        P("ctx", "mp"),
        P("ctx", "mp"),
        P("ctx", "mp"),
        P("mp", None),
        P(None, "mp"),
        P("ctx", "mp"),
    )
    return jax.shard_map(
        per_device,
        mesh=mesh,
        in_specs=placed,
        out_specs=(P("ctx", "mp"), P("ctx", "mp"), P("ctx", "mp"), P("ctx", "mp"), P("ctx", "mp")),
        check_vma=False,
    )
```

profile of v0, /device:TPU:8, one launch (start us, length us, event | category | flops | bytes accessed | tf_op | source)
XLA Modules:
  0.0 188.9 jit_solution(1581389626179336944)
XLA Ops:
  9.5 4.3 %collective-permute-start = (bf16[2,128,512]{1,2,0:T(8,128)(2,1)S(1)}, bf16[2,128,512]{1,2,0:T(8,128)(2,1)S(1)}, u32[]{:S(2)}, u32[]{:S(2)}) collective-permute-start(bf16[2,128,512]{1,2,0:T(8,128)(2,1)S(1)} %pad_maximum_fusion.1), channel_id=1, source_target_pairs={{0,4},{4,8},{8,12},{12,16},{16,20},{20,24},{24,28},{28,32},{32,36}... | collective-permute-start | bytes 786440 | tf_op jit(solution)/shard_map/ppermute | solution.py:14
  13.7 10.7 %collective-permute-start.2 = (bf16[2,128,512]{1,2,0:T(8,128)(2,1)S(1)}, bf16[2,128,512]{1,2,0:T(8,128)(2,1)S(1)}, u32[]{:S(2)}, u32[]{:S(2)}) collective-permute-start(bf16[2,128,512]{1,2,0:T(8,128)(2,1)S(1)} %pad_maximum_fusion.1), channel_id=1, source_target_pairs={{4,0},{8,4},{12,8},{16,12},{20,16},{24,20},{28,24},{32,28},{36,32}... | collective-permute-start | bytes 786440 | tf_op jit(solution)/shard_map/ppermute | solution.py:14
  24.4 4.4 %collective-permute-done = bf16[2,128,512]{1,2,0:T(8,128)(2,1)S(1)} collective-permute-done((bf16[2,128,512]{1,2,0:T(8,128)(2,1)S(1)}, bf16[2,128,512]{1,2,0:T(8,128)(2,1)S(1)}, u32[]{:S(2)}, u32[]{:S(2)}) %collective-permute-start) | collective-permute-done | bytes 262176 | tf_op jit(solution)/shard_map/ppermute | solution.py:14
  28.8 1.9 %collective-permute-start.1 = (bf16[2,128,512]{1,2,0:T(8,128)(2,1)S(1)}, bf16[2,128,512]{1,2,0:T(8,128)(2,1)S(1)}, u32[]{:S(2)}, u32[]{:S(2)}) collective-permute-start(bf16[2,128,512]{1,2,0:T(8,128)(2,1)S(1)} %collective-permute-done), channel_id=1, source_target_pairs={{0,4},{4,8},{8,12},{12,16},{16,20},{20,24},{24,28},{28,32},{32,36}... | collective-permute-start | bytes 786440 | tf_op jit(solution)/shard_map/ppermute | solution.py:14
  31.8 8.1 %collective-permute-start.3 = (bf16[2,128,512]{1,2,0:T(8,128)(2,1)S(1)}, bf16[2,128,512]{1,2,0:T(8,128)(2,1)S(1)}, u32[]{:S(2)}, u32[]{:S(2)}) collective-permute-start(bf16[2,128,512]{1,2,0:T(8,128)(2,1)S(1)} %collective-permute-done.2), channel_id=1, source_target_pairs={{4,0},{8,4},{12,8},{16,12},{20,16},{24,20},{28,24},{32,28},{36,32}... | collective-permute-start | bytes 786440 | tf_op jit(solution)/shard_map/ppermute | solution.py:14
  39.9 2.5 %collective-permute-done.1 = bf16[2,128,512]{1,2,0:T(8,128)(2,1)S(1)} collective-permute-done((bf16[2,128,512]{1,2,0:T(8,128)(2,1)S(1)}, bf16[2,128,512]{1,2,0:T(8,128)(2,1)S(1)}, u32[]{:S(2)}, u32[]{:S(2)}) %collective-permute-start.1) | collective-permute-done | bytes 262176 | tf_op jit(solution)/shard_map/ppermute | solution.py:14
  42.6 2.0 %collective-permute-done.3 = bf16[2,128,512]{1,2,0:T(8,128)(2,1)S(1)} collective-permute-done((bf16[2,128,512]{1,2,0:T(8,128)(2,1)S(1)}, bf16[2,128,512]{1,2,0:T(8,128)(2,1)S(1)}, u32[]{:S(2)}, u32[]{:S(2)}) %collective-permute-start.3) | collective-permute-done | bytes 262176 | tf_op jit(solution)/shard_map/ppermute | solution.py:14
  48.2 1.8 fusion.96
  50.0 41.9 %reduce-scatter.2.cloned.1.call-done = bf16[128,512]{1,0:T(8,128)(2,1)} async-done(((bf16[128,2048]{1,0:T(8,128)(2,1)}), bf16[128,512]{1,0:T(8,128)(2,1)}) %reduce-scatter.2.cloned.1.call-update) | async-done | bytes 131088 | tf_op jit(solution)/shard_map/reduce_scatter | solution.py:84
  93.0 3.6 %collective-permute-start.4 = (bf16[15,512]{1,0:T(8,128)(2,1)S(1)}, bf16[15,512]{1,0:T(8,128)(2,1)S(1)}, u32[]{:S(2)}, u32[]{:S(2)}) collective-permute-start(bf16[15,512]{1,0:T(8,128)(2,1)S(1)} %get-tuple-element.27), channel_id=1, source_target_pairs={{0,4},{4,8},{8,12},{12,16},{16,20},{20,24},{24,28},{28,32},{32,36}... | collective-permute-start | bytes 46088 | tf_op jit(solution)/shard_map/ppermute | solution.py:22
  96.5 6.5 %collective-permute-start.5 = (bf16[15,512]{1,0:T(8,128)(2,1)S(1)}, bf16[15,512]{1,0:T(8,128)(2,1)S(1)}, u32[]{:S(2)}, u32[]{:S(2)}) collective-permute-start(bf16[15,512]{1,0:T(8,128)(2,1)S(1)} %get-tuple-element.28), channel_id=1, source_target_pairs={{4,0},{8,4},{12,8},{16,12},{20,16},{24,20},{28,24},{32,28},{36,32}... | collective-permute-start | bytes 46088 | tf_op jit(solution)/shard_map/ppermute | solution.py:25
  104.7 2.3 %fusion.17 = (bf16[128,512]{1,0:T(8,128)(2,1)S(1)}, f32[128,512]{1,0:T(8,128)}) fusion(bf16[128,512]{1,0:T(8,128)(2,1)S(1)} %copy-done.14, f32[158,512]{1,0:T(8,128)S(1)} %maximum_convert_fusion, f32[512]{0:T(512)S(1)} %bitcast.146, f32[512]{0:T(512)S(1)} %bitcast.148, f32[512]{0:T(512)S(1)} %bitcast.90, f32[512]{0:T(512)S(1)} %bitcast.92, f32[512]{0:T(512)} %bitcast.94, ...), kind=kLoop, calls=%fused_computation.34 | loop fusion | flops 4653056 | bytes 8714240 | tf_op jit(solution)/shard_map/convert_element_type | solution.py:100
  107.0 1.9 %collective-permute-start.6 = (bf16[15,512]{1,0:T(8,128)(2,1)S(1)}, bf16[15,512]{1,0:T(8,128)(2,1)S(1)}, u32[]{:S(2)}, u32[]{:S(2)}) collective-permute-start(bf16[15,512]{1,0:T(8,128)(2,1)S(1)} %get-tuple-element.25), channel_id=1, source_target_pairs={{0,4},{4,8},{8,12},{12,16},{16,20},{20,24},{24,28},{28,32},{32,36}... | collective-permute-start | bytes 46088 | tf_op jit(solution)/shard_map/ppermute | solution.py:22
  108.9 8.4 %collective-permute-start.7 = (bf16[15,512]{1,0:T(8,128)(2,1)S(1)}, bf16[15,512]{1,0:T(8,128)(2,1)S(1)}, u32[]{:S(2)}, u32[]{:S(2)}) collective-permute-start(bf16[15,512]{1,0:T(8,128)(2,1)S(1)} %get-tuple-element.26), channel_id=1, source_target_pairs={{4,0},{8,4},{12,8},{16,12},{20,16},{24,20},{28,24},{32,28},{36,32}... | collective-permute-start | bytes 46088 | tf_op jit(solution)/shard_map/ppermute | solution.py:25
  119.8 11.3 %all_gather.3 = bf16[128,2048]{1,0:T(8,128)(2,1)S(1)} all-gather(bf16[128,512]{1,0:T(8,128)(2,1)S(1)} %fusion.44), channel_id=1, replica_groups=mesh['ctx'=128,'mp'=4] {'mp'}, dimensions={1}, use_global_device_ids=true | all-gather | bytes 655360 | tf_op jit(solution)/shard_map/all_gather | solution.py:111
  137.4 1.7 copy.41
  139.1 2.5 %fusion.99 = f32[4,640,128]{1,2,0:T(8,128)} fusion(bf16[4,128,640]{1,2,0:T(8,128)(2,1)} %fusion.5, bf16[128,4,128]{0,2,1:T(8,128)(2,1)S(1)} %bitcast.81), kind=kOutput, calls=%fused_computation.194 | convolution fusion | flops 83886080 | bytes 2097152 | tf_op jit(solution)/shard_map/hqk,qhd->khd/dot_general | solution.py:125
  141.7 2.8 %copy.40 = f32[1,640,512]{2,1,0:T(8,128)} copy(f32[1,640,512]{1,2,0:T(8,128)} %bitcast.77) | data formatting | bytes 2621440 | tf_op jit(solution)/shard_map/stack;reshape | solution.py:131
  146.2 1.9 %collective-permute-start.8 = (bf16[2,128,512]{2,1,0:T(8,128)(2,1)S(1)}, bf16[2,128,512]{2,1,0:T(8,128)(2,1)S(1)}, u32[]{:S(2)}, u32[]{:S(2)}) collective-permute-start(bf16[2,128,512]{2,1,0:T(8,128)(2,1)S(1)} %get-tuple-element.19), channel_id=1, source_target_pairs={{0,4},{4,8},{8,12},{12,16},{16,20},{20,24},{24,28},{28,32},{32,36}... | collective-permute-start | bytes 786440 | tf_op jit(solution)/shard_map/ppermute | solution.py:14
  148.1 8.8 %collective-permute-start.10 = (bf16[2,128,512]{2,1,0:T(8,128)(2,1)S(1)}, bf16[2,128,512]{2,1,0:T(8,128)(2,1)S(1)}, u32[]{:S(2)}, u32[]{:S(2)}) collective-permute-start(bf16[2,128,512]{2,1,0:T(8,128)(2,1)S(1)} %get-tuple-element.20), channel_id=1, source_target_pairs={{4,0},{8,4},{12,8},{16,12},{20,16},{24,20},{28,24},{32,28},{36,32}... | collective-permute-start | bytes 786440 | tf_op jit(solution)/shard_map/ppermute | solution.py:14
  157.0 4.7 %collective-permute-done.8 = bf16[2,128,512]{2,1,0:T(8,128)(2,1)S(1)} collective-permute-done((bf16[2,128,512]{2,1,0:T(8,128)(2,1)S(1)}, bf16[2,128,512]{2,1,0:T(8,128)(2,1)S(1)}, u32[]{:S(2)}, u32[]{:S(2)}) %collective-permute-start.8) | collective-permute-done | bytes 262176 | tf_op jit(solution)/shard_map/ppermute | solution.py:14
  164.0 1.9 %collective-permute-start.9 = (bf16[2,128,512]{2,1,0:T(8,128)(2,1)}, bf16[2,128,512]{2,1,0:T(8,128)(2,1)}, u32[]{:S(2)}, u32[]{:S(2)}) collective-permute-start(bf16[2,128,512]{2,1,0:T(8,128)(2,1)} %get-tuple-element.17), channel_id=1, source_target_pairs={{0,4},{4,8},{8,12},{12,16},{16,20},{20,24},{24,28},{28,32},{32,36}... | collective-permute-start | bytes 786440 | tf_op jit(solution)/shard_map/ppermute | solution.py:14
  165.9 8.6 %collective-permute-start.11 = (bf16[2,128,512]{2,1,0:T(8,128)(2,1)}, bf16[2,128,512]{2,1,0:T(8,128)(2,1)}, u32[]{:S(2)}, u32[]{:S(2)}) collective-permute-start(bf16[2,128,512]{2,1,0:T(8,128)(2,1)} %get-tuple-element.18), channel_id=1, source_target_pairs={{4,0},{8,4},{12,8},{16,12},{20,16},{24,20},{28,24},{32,28},{36,32}... | collective-permute-start | bytes 786440 | tf_op jit(solution)/shard_map/ppermute | solution.py:14
  176.4 2.5 %collective-permute-done.9 = bf16[2,128,512]{2,1,0:T(8,128)(2,1)} collective-permute-done((bf16[2,128,512]{2,1,0:T(8,128)(2,1)}, bf16[2,128,512]{2,1,0:T(8,128)(2,1)}, u32[]{:S(2)}, u32[]{:S(2)}) %collective-permute-start.9) | collective-permute-done | bytes 262176 | tf_op jit(solution)/shard_map/ppermute | solution.py:14
  (107 shorter events, 27.1 us)
Async XLA Ops:
  7.2 39.7 %copy-start = (bf16[512,2048]{1,0:T(8,128)(2,1)S(1)}, bf16[512,2048]{1,0:T(8,128)(2,1)}, u32[]{:S(2)}) copy-start(bf16[512,2048]{1,0:T(8,128)(2,1)} %param.11) | copy-start | bytes 6291460
  7.2 84.8 %reduce-scatter.2.cloned.1.call-start = ((), (), s32[]{:S(2)}) async-start(), calls=%async_computation.1 | async-start | bytes 655360 | tf_op jit(solution)/shard_map/reduce_scatter | solution.py:84
  9.5 19.3 %collective-permute-start = (bf16[2,128,512]{1,2,0:T(8,128)(2,1)S(1)}, bf16[2,128,512]{1,2,0:T(8,128)(2,1)S(1)}, u32[]{:S(2)}, u32[]{:S(2)}) collective-permute-start(bf16[2,128,512]{1,2,0:T(8,128)(2,1)S(1)} %pad_maximum_fusion.1), channel_id=1, source_target_pairs={{0,4},{4,8},{8,12},{12,16},{16,20},{20,24},{24,28},{28,32},{32,36}... | collective-permute-start | bytes 786440 | tf_op jit(solution)/shard_map/ppermute | solution.py:14
  13.7 18.0 %collective-permute-start.2 = (bf16[2,128,512]{1,2,0:T(8,128)(2,1)S(1)}, bf16[2,128,512]{1,2,0:T(8,128)(2,1)S(1)}, u32[]{:S(2)}, u32[]{:S(2)}) collective-permute-start(bf16[2,128,512]{1,2,0:T(8,128)(2,1)S(1)} %pad_maximum_fusion.1), channel_id=1, source_target_pairs={{4,0},{8,4},{12,8},{16,12},{20,16},{24,20},{28,24},{32,28},{36,32}... | collective-permute-start | bytes 786440 | tf_op jit(solution)/shard_map/ppermute | solution.py:14
  28.8 13.6 %collective-permute-start.1 = (bf16[2,128,512]{1,2,0:T(8,128)(2,1)S(1)}, bf16[2,128,512]{1,2,0:T(8,128)(2,1)S(1)}, u32[]{:S(2)}, u32[]{:S(2)}) collective-permute-start(bf16[2,128,512]{1,2,0:T(8,128)(2,1)S(1)} %collective-permute-done), channel_id=1, source_target_pairs={{0,4},{4,8},{8,12},{12,16},{16,20},{20,24},{24,28},{28,32},{32,36}... | collective-permute-start | bytes 786440 | tf_op jit(solution)/shard_map/ppermute | solution.py:14
  31.8 12.9 %collective-permute-start.3 = (bf16[2,128,512]{1,2,0:T(8,128)(2,1)S(1)}, bf16[2,128,512]{1,2,0:T(8,128)(2,1)S(1)}, u32[]{:S(2)}, u32[]{:S(2)}) collective-permute-start(bf16[2,128,512]{1,2,0:T(8,128)(2,1)S(1)} %collective-permute-done.2), channel_id=1, source_target_pairs={{4,0},{8,4},{12,8},{16,12},{20,16},{24,20},{28,24},{32,28},{36,32}... | collective-permute-start | bytes 786440 | tf_op jit(solution)/shard_map/ppermute | solution.py:14
  48.2 56.3 %copy-start.14 = (bf16[128,512]{1,0:T(8,128)(2,1)S(1)}, bf16[128,512]{1,0:T(8,128)(2,1)}, u32[]{:S(2)}) copy-start(bf16[128,512]{1,0:T(8,128)(2,1)} %param.13) | copy-start | bytes 393220
  93.0 11.1 %collective-permute-start.4 = (bf16[15,512]{1,0:T(8,128)(2,1)S(1)}, bf16[15,512]{1,0:T(8,128)(2,1)S(1)}, u32[]{:S(2)}, u32[]{:S(2)}) collective-permute-start(bf16[15,512]{1,0:T(8,128)(2,1)S(1)} %get-tuple-element.27), channel_id=1, source_target_pairs={{0,4},{4,8},{8,12},{12,16},{16,20},{20,24},{24,28},{28,32},{32,36}... | collective-permute-start | bytes 46088 | tf_op jit(solution)/shard_map/ppermute | solution.py:22
  96.5 7.9 %collective-permute-start.5 = (bf16[15,512]{1,0:T(8,128)(2,1)S(1)}, bf16[15,512]{1,0:T(8,128)(2,1)S(1)}, u32[]{:S(2)}, u32[]{:S(2)}) collective-permute-start(bf16[15,512]{1,0:T(8,128)(2,1)S(1)} %get-tuple-element.28), channel_id=1, source_target_pairs={{4,0},{8,4},{12,8},{16,12},{20,16},{24,20},{28,24},{32,28},{36,32}... | collective-permute-start | bytes 46088 | tf_op jit(solution)/shard_map/ppermute | solution.py:25
  104.5 14.3 %copy-start.15 = (f32[1,512]{1,0:T(1,128)S(1)}, f32[1,512]{1,0:T(1,128)}, u32[]{:S(2)}) copy-start(f32[1,512]{1,0:T(1,128)} %get-tuple-element.32) | copy-start | bytes 6148
  104.5 14.3 %copy-start.16 = (f32[1,512]{1,0:T(1,128)S(1)}, f32[1,512]{1,0:T(1,128)}, u32[]{:S(2)}) copy-start(f32[1,512]{1,0:T(1,128)} %get-tuple-element.33) | copy-start | bytes 6148
  104.6 14.3 %copy-start.17 = (f32[1,512]{1,0:T(1,128)S(1)}, f32[1,512]{1,0:T(1,128)}, u32[]{:S(2)}) copy-start(f32[1,512]{1,0:T(1,128)} %get-tuple-element.34) | copy-start | bytes 6148
  104.6 14.3 %copy-start.18 = (f32[1,512]{1,0:T(1,128)S(1)}, f32[1,512]{1,0:T(1,128)}, u32[]{:S(2)}) copy-start(f32[1,512]{1,0:T(1,128)} %get-tuple-element.35) | copy-start | bytes 6148
  107.0 10.4 %collective-permute-start.6 = (bf16[15,512]{1,0:T(8,128)(2,1)S(1)}, bf16[15,512]{1,0:T(8,128)(2,1)S(1)}, u32[]{:S(2)}, u32[]{:S(2)}) collective-permute-start(bf16[15,512]{1,0:T(8,128)(2,1)S(1)} %get-tuple-element.25), channel_id=1, source_target_pairs={{0,4},{4,8},{8,12},{12,16},{16,20},{20,24},{24,28},{28,32},{32,36}... | collective-permute-start | bytes 46088 | tf_op jit(solution)/shard_map/ppermute | solution.py:22
  108.9 9.9 %collective-permute-start.7 = (bf16[15,512]{1,0:T(8,128)(2,1)S(1)}, bf16[15,512]{1,0:T(8,128)(2,1)S(1)}, u32[]{:S(2)}, u32[]{:S(2)}) collective-permute-start(bf16[15,512]{1,0:T(8,128)(2,1)S(1)} %get-tuple-element.26), channel_id=1, source_target_pairs={{4,0},{8,4},{12,8},{16,12},{20,16},{24,20},{28,24},{32,28},{36,32}... | collective-permute-start | bytes 46088 | tf_op jit(solution)/shard_map/ppermute | solution.py:25
  144.5 18.6 %copy-start.1 = (f32[1,640,512]{2,1,0:T(8,128)S(1)}, f32[1,640,512]{2,1,0:T(8,128)}, u32[]{:S(2)}) copy-start(f32[1,640,512]{2,1,0:T(8,128)} %copy.40) | copy-start | bytes 3932164
  146.2 15.5 %collective-permute-start.8 = (bf16[2,128,512]{2,1,0:T(8,128)(2,1)S(1)}, bf16[2,128,512]{2,1,0:T(8,128)(2,1)S(1)}, u32[]{:S(2)}, u32[]{:S(2)}) collective-permute-start(bf16[2,128,512]{2,1,0:T(8,128)(2,1)S(1)} %get-tuple-element.19), channel_id=1, source_target_pairs={{0,4},{4,8},{8,12},{12,16},{16,20},{20,24},{24,28},{28,32},{32,36}... | collective-permute-start | bytes 786440 | tf_op jit(solution)/shard_map/ppermute | solution.py:14
  148.1 26.5 %copy-start.8 = (bf16[128,512]{1,0:T(8,128)(2,1)S(1)}, bf16[128,512]{1,0:T(8,128)(2,1)}, u32[]{:S(2)}) copy-start(bf16[128,512]{1,0:T(8,128)(2,1)} %copy-done.7) | copy-start | bytes 393220
  148.1 26.5 %copy-start.12 = (f32[128,512]{1,0:T(8,128)S(1)}, f32[128,512]{1,0:T(8,128)}, u32[]{:S(2)}) copy-start(f32[128,512]{1,0:T(8,128)} %get-tuple-element.16) | copy-start | bytes 786436
  148.1 27.2 %copy-start.3 = (bf16[1,640,512]{1,2,0:T(8,128)(2,1)S(1)}, bf16[1,640,512]{1,2,0:T(8,128)(2,1)}, u32[]{:S(2)}) copy-start(bf16[1,640,512]{1,2,0:T(8,128)(2,1)} %copy-done.2) | copy-start | bytes 1966084
  148.1 27.2 %copy-start.6 = (bf16[4,128,640]{1,2,0:T(8,128)(2,1)S(1)}, bf16[4,128,640]{1,2,0:T(8,128)(2,1)}, u32[]{:S(2)}) copy-start(bf16[4,128,640]{1,2,0:T(8,128)(2,1)} %fusion.5) | copy-start | bytes 1966084
  148.1 14.9 %collective-permute-start.10 = (bf16[2,128,512]{2,1,0:T(8,128)(2,1)S(1)}, bf16[2,128,512]{2,1,0:T(8,128)(2,1)S(1)}, u32[]{:S(2)}, u32[]{:S(2)}) collective-permute-start(bf16[2,128,512]{2,1,0:T(8,128)(2,1)S(1)} %get-tuple-element.20), channel_id=1, source_target_pairs={{4,0},{8,4},{12,8},{16,12},{20,16},{24,20},{28,24},{32,28},{36,32}... | collective-permute-start | bytes 786440 | tf_op jit(solution)/shard_map/ppermute | solution.py:14
  164.0 14.9 %collective-permute-start.9 = (bf16[2,128,512]{2,1,0:T(8,128)(2,1)}, bf16[2,128,512]{2,1,0:T(8,128)(2,1)}, u32[]{:S(2)}, u32[]{:S(2)}) collective-permute-start(bf16[2,128,512]{2,1,0:T(8,128)(2,1)} %get-tuple-element.17), channel_id=1, source_target_pairs={{0,4},{4,8},{8,12},{12,16},{16,20},{20,24},{24,28},{28,32},{32,36}... | collective-permute-start | bytes 786440 | tf_op jit(solution)/shard_map/ppermute | solution.py:14
  165.9 14.2 %collective-permute-start.11 = (bf16[2,128,512]{2,1,0:T(8,128)(2,1)}, bf16[2,128,512]{2,1,0:T(8,128)(2,1)}, u32[]{:S(2)}, u32[]{:S(2)}) collective-permute-start(bf16[2,128,512]{2,1,0:T(8,128)(2,1)} %get-tuple-element.18), channel_id=1, source_target_pairs={{4,0},{8,4},{12,8},{16,12},{20,16},{24,20},{28,24},{32,28},{36,32}... | collective-permute-start | bytes 786440 | tf_op jit(solution)/shard_map/ppermute | solution.py:14
  (20 other events, 213.0 us)
Sparse Core Ops, SparseCore 0:
  48.3 43.5 reduce-scatter.1
where the time goes:
time: 190 us; the launch traced here: 189 us
  starting transfers between devices  66.7 us (35%)
  waiting for transfers between devices  62.3 us (33%)
  between operations  14.7 us (8%)
  local copies, waits for them, and re-layouts  14.6 us (8%)
  blocking collectives  11.3 us (6%)
  other arithmetic  9.99 us (5%)
  matrix products  9.27 us (5%)
    ppermute x8, starting transfers between devices, shifted(): return lax.ppermute(block, axis, route)  46.3 us
    reduce_scatter x1, waiting for transfers between devices, per_device(): lax.psum_scatter(partial_out.astype(jnp.bfloat16), 'mp', scatter_dimensio...  41.9 us
    ppermute x8, waiting for transfers between devices, shifted(): return lax.ppermute(block, axis, route)  18.6 us
    ppermute x2, starting transfers between devices, with_halo(): lax.ppermute(lax.slice_in_dim(block, 0, width, axis=dim), axis, backward)  14.9 us
    all_gather x1, blocking collectives, per_device(): lax.all_gather(grad_input, 'mp', axis=1, tiled=True)  11.3 us
    ppermute x2, starting transfers between devices, with_halo(): lax.ppermute(lax.slice_in_dim(block, block.shape[dim] - width, None, axis...  5.47 us
    another operation x2, local copies, waits for them, and re-layouts, per_device(): jnp.stack([key_parts.reshape(window_len, local_width), value_parts.reshap...  4.56 us
    unnamed x68, local copies, waits for them, and re-layouts  4.26 us
  transfers between devices with their start and end apart: 13, of which 10 were waited for; matrix products, arithmetic and copies ran while one was open for 3% of the time, Pallas kernels for 0%

commit v1 on v0

--- a/solution.py
+++ b/solution.py
@@ -106,11 +106,17 @@
             grad_hidden + kernel[tap_index][None, :] * grad_pad[first_row : first_row + frames]
         )
     grad_input = grad_hidden.astype(jnp.bfloat16)
+    sheets_fix = lambda a0, peer_axis: jnp.concatenate(
+        lax.all_to_all(
+            jnp.stack([a0] * lax.axis_size(peer_axis), axis=0),
+            axis_name=peer_axis,
+            split_axis=0,
+            concat_axis=0,
+        ),
+        axis=1,
+    )
     upstream = jnp.einsum(
-        "rn,wn->rw",
-        lax.all_gather(grad_input, "mp", axis=1, tiled=True),
-        out_weight,
-        preferred_element_type=jnp.float32,
+        "rn,wn->rw", sheets_fix(grad_input, "mp"), out_weight, preferred_element_type=jnp.float32
     ).astype(jnp.bfloat16)
     up_heads = upstream.reshape(frames, local_heads, HDIM)
     row_delta = jnp.sum(up_heads.astype(jnp.float32) * attended.astype(jnp.float32), axis=2).T

time: 190 us -> 200 us (1.053)
  the two profiles are of different devices: /device:TPU:8 before, /device:TPU:24 now
where the time goes in v1:
time: 200 us; the launch traced here: 199 us
  starting transfers between devices  69.6 us (35%)
  waiting for transfers between devices  58.7 us (29%)
  blocking collectives  20 us (10%)
  local copies, waits for them, and re-layouts  16.4 us (8%)
  between operations  14.7 us (7%)
  other arithmetic  10 us (5%)
  matrix products  9.28 us (5%)
    ppermute x8, starting transfers between devices, shifted(): return lax.ppermute(block, axis, route)  47.7 us
    reduce_scatter x1, waiting for transfers between devices, per_device(): lax.psum_scatter(partial_out.astype(jnp.bfloat16), 'mp', scatter_dimensio...  39.2 us
    all_to_all x1, blocking collectives, per_device(): lax.all_to_all(jnp.stack([a0] * lax.axis_size(peer_axis), axis=0), axis_n...  20 us
    ppermute x8, waiting for transfers between devices, shifted(): return lax.ppermute(block, axis, route)  17.6 us
    ppermute x2, starting transfers between devices, with_halo(): lax.ppermute(lax.slice_in_dim(block, 0, width, axis=dim), axis, backward)  16.4 us
    ppermute x2, starting transfers between devices, with_halo(): lax.ppermute(lax.slice_in_dim(block, block.shape[dim] - width, None, axis...  5.48 us
    another operation x2, local copies, waits for them, and re-layouts, per_device(): jnp.stack([key_parts.reshape(window_len, local_width), value_parts.reshap...  4.58 us
    unnamed x70, local copies, waits for them, and re-layouts  4.28 us
  transfers between devices with their start and end apart: 13, of which 10 were waited for; matrix products, arithmetic and copies ran while one was open for 3% of the time, Pallas kernels for 0%

profile of v1, /device:TPU:24, one launch (start us, length us, event | category | flops | bytes accessed | tf_op | source)
XLA Modules:
  0.0 198.7 jit_solution(3512670142833875977)
XLA Ops:
  9.5 4.3 %collective-permute-start = (bf16[2,128,512]{1,2,0:T(8,128)(2,1)S(1)}, bf16[2,128,512]{1,2,0:T(8,128)(2,1)S(1)}, u32[]{:S(2)}, u32[]{:S(2)}) collective-permute-start(bf16[2,128,512]{1,2,0:T(8,128)(2,1)S(1)} %pad_maximum_fusion.1), channel_id=1, source_target_pairs={{0,4},{4,8},{8,12},{12,16},{16,20},{20,24},{24,28},{28,32},{32,36}... | collective-permute-start | bytes 786440 | tf_op jit(solution)/shard_map/ppermute | solution.py:14
  13.7 10.7 %collective-permute-start.2 = (bf16[2,128,512]{1,2,0:T(8,128)(2,1)S(1)}, bf16[2,128,512]{1,2,0:T(8,128)(2,1)S(1)}, u32[]{:S(2)}, u32[]{:S(2)}) collective-permute-start(bf16[2,128,512]{1,2,0:T(8,128)(2,1)S(1)} %pad_maximum_fusion.1), channel_id=1, source_target_pairs={{4,0},{8,4},{12,8},{16,12},{20,16},{24,20},{28,24},{32,28},{36,32}... | collective-permute-start | bytes 786440 | tf_op jit(solution)/shard_map/ppermute | solution.py:14
  24.4 4.4 %collective-permute-done = bf16[2,128,512]{1,2,0:T(8,128)(2,1)S(1)} collective-permute-done((bf16[2,128,512]{1,2,0:T(8,128)(2,1)S(1)}, bf16[2,128,512]{1,2,0:T(8,128)(2,1)S(1)}, u32[]{:S(2)}, u32[]{:S(2)}) %collective-permute-start) | collective-permute-done | bytes 262176 | tf_op jit(solution)/shard_map/ppermute | solution.py:14
  28.8 1.9 collective-permute-start.1
  31.8 8.1 %collective-permute-start.3 = (bf16[2,128,512]{1,2,0:T(8,128)(2,1)S(1)}, bf16[2,128,512]{1,2,0:T(8,128)(2,1)S(1)}, u32[]{:S(2)}, u32[]{:S(2)}) collective-permute-start(bf16[2,128,512]{1,2,0:T(8,128)(2,1)S(1)} %collective-permute-done.2), channel_id=1, source_target_pairs={{4,0},{8,4},{12,8},{16,12},{20,16},{24,20},{28,24},{32,28},{36,32}... | collective-permute-start | bytes 786440 | tf_op jit(solution)/shard_map/ppermute | solution.py:14
  39.9 2.5 %collective-permute-done.1 = bf16[2,128,512]{1,2,0:T(8,128)(2,1)S(1)} collective-permute-done((bf16[2,128,512]{1,2,0:T(8,128)(2,1)S(1)}, bf16[2,128,512]{1,2,0:T(8,128)(2,1)S(1)}, u32[]{:S(2)}, u32[]{:S(2)}) %collective-permute-start.1) | collective-permute-done | bytes 262176 | tf_op jit(solution)/shard_map/ppermute | solution.py:14
  42.6 2.0 %collective-permute-done.3 = bf16[2,128,512]{1,2,0:T(8,128)(2,1)S(1)} collective-permute-done((bf16[2,128,512]{1,2,0:T(8,128)(2,1)S(1)}, bf16[2,128,512]{1,2,0:T(8,128)(2,1)S(1)}, u32[]{:S(2)}, u32[]{:S(2)}) %collective-permute-start.3) | collective-permute-done | bytes 262176 | tf_op jit(solution)/shard_map/ppermute | solution.py:14
  48.2 1.8 fusion.96
  50.0 39.2 %reduce-scatter.2.cloned.1.call-done = bf16[128,512]{1,0:T(8,128)(2,1)} async-done(((bf16[128,2048]{1,0:T(8,128)(2,1)}), bf16[128,512]{1,0:T(8,128)(2,1)}) %reduce-scatter.2.cloned.1.call-update) | async-done | bytes 131088 | tf_op jit(solution)/shard_map/reduce_scatter | solution.py:84
  90.2 3.6 %collective-permute-start.4 = (bf16[15,512]{1,0:T(8,128)(2,1)S(1)}, bf16[15,512]{1,0:T(8,128)(2,1)S(1)}, u32[]{:S(2)}, u32[]{:S(2)}) collective-permute-start(bf16[15,512]{1,0:T(8,128)(2,1)S(1)} %get-tuple-element.27), channel_id=1, source_target_pairs={{0,4},{4,8},{8,12},{12,16},{16,20},{20,24},{24,28},{28,32},{32,36}... | collective-permute-start | bytes 46088 | tf_op jit(solution)/shard_map/ppermute | solution.py:22
  93.8 8.0 %collective-permute-start.5 = (bf16[15,512]{1,0:T(8,128)(2,1)S(1)}, bf16[15,512]{1,0:T(8,128)(2,1)S(1)}, u32[]{:S(2)}, u32[]{:S(2)}) collective-permute-start(bf16[15,512]{1,0:T(8,128)(2,1)S(1)} %get-tuple-element.28), channel_id=1, source_target_pairs={{4,0},{8,4},{12,8},{16,12},{20,16},{24,20},{28,24},{32,28},{36,32}... | collective-permute-start | bytes 46088 | tf_op jit(solution)/shard_map/ppermute | solution.py:25
  103.5 2.3 %fusion.17 = (bf16[128,512]{1,0:T(8,128)(2,1)S(1)}, f32[128,512]{1,0:T(8,128)}) fusion(bf16[128,512]{1,0:T(8,128)(2,1)S(1)} %copy-done.14, f32[158,512]{1,0:T(8,128)S(1)} %maximum_convert_fusion, f32[512]{0:T(512)S(1)} %bitcast.150, f32[512]{0:T(512)S(1)} %bitcast.152, f32[512]{0:T(512)S(1)} %bitcast.94, f32[512]{0:T(512)S(1)} %bitcast.96, f32[512]{0:T(512)} %bitcast.98, ...), kind=kLoop, calls=%fused_computation.34 | loop fusion | flops 4653056 | bytes 8714240 | tf_op jit(solution)/shard_map/convert_element_type | solution.py:100
  105.8 1.9 collective-permute-start.6
  107.7 8.4 %collective-permute-start.7 = (bf16[15,512]{1,0:T(8,128)(2,1)S(1)}, bf16[15,512]{1,0:T(8,128)(2,1)S(1)}, u32[]{:S(2)}, u32[]{:S(2)}) collective-permute-start(bf16[15,512]{1,0:T(8,128)(2,1)S(1)} %get-tuple-element.26), channel_id=1, source_target_pairs={{4,0},{8,4},{12,8},{16,12},{20,16},{24,20},{28,24},{32,28},{36,32}... | collective-permute-start | bytes 46088 | tf_op jit(solution)/shard_map/ppermute | solution.py:25
  120.3 20.0 %all_to_all.5 = bf16[4,128,512]{1,2,0:T(8,128)(2,1)S(1)} all-to-all(bf16[4,128,512]{1,2,0:T(8,128)(2,1)S(1)} %stack.22), channel_id=1, replica_groups=mesh['ctx'=128,'mp'=4] {'mp'}, dimensions={0} | all-to-all | bytes 1048576 | tf_op jit(solution)/shard_map/all_to_all | solution.py:110
  146.7 1.7 copy.42
  148.5 2.5 %fusion.99 = f32[4,640,128]{1,2,0:T(8,128)} fusion(bf16[4,128,640]{1,2,0:T(8,128)(2,1)} %fusion.5, bf16[128,4,128]{0,2,1:T(8,128)(2,1)S(1)} %bitcast.85), kind=kOutput, calls=%fused_computation.194 | convolution fusion | flops 83886080 | bytes 2097152 | tf_op jit(solution)/shard_map/hqk,qhd->khd/dot_general | solution.py:131
  151.0 2.8 %copy.41 = f32[1,640,512]{2,1,0:T(8,128)} copy(f32[1,640,512]{1,2,0:T(8,128)} %bitcast.80) | data formatting | bytes 2621440 | tf_op jit(solution)/shard_map/stack;reshape | solution.py:137
  155.5 1.9 collective-permute-start.8
  157.5 10.3 %collective-permute-start.10 = (bf16[2,128,512]{2,1,0:T(8,128)(2,1)S(1)}, bf16[2,128,512]{2,1,0:T(8,128)(2,1)S(1)}, u32[]{:S(2)}, u32[]{:S(2)}) collective-permute-start(bf16[2,128,512]{2,1,0:T(8,128)(2,1)S(1)} %get-tuple-element.20), channel_id=1, source_target_pairs={{4,0},{8,4},{12,8},{16,12},{20,16},{24,20},{28,24},{32,28},{36,32}... | collective-permute-start | bytes 786440 | tf_op jit(solution)/shard_map/ppermute | solution.py:14
  167.7 4.3 %collective-permute-done.8 = bf16[2,128,512]{2,1,0:T(8,128)(2,1)S(1)} collective-permute-done((bf16[2,128,512]{2,1,0:T(8,128)(2,1)S(1)}, bf16[2,128,512]{2,1,0:T(8,128)(2,1)S(1)}, u32[]{:S(2)}, u32[]{:S(2)}) %collective-permute-start.8) | collective-permute-done | bytes 262176 | tf_op jit(solution)/shard_map/ppermute | solution.py:14
  174.3 1.9 collective-permute-start.9
  176.2 8.6 %collective-permute-start.11 = (bf16[2,128,512]{2,1,0:T(8,128)(2,1)}, bf16[2,128,512]{2,1,0:T(8,128)(2,1)}, u32[]{:S(2)}, u32[]{:S(2)}) collective-permute-start(bf16[2,128,512]{2,1,0:T(8,128)(2,1)} %get-tuple-element.18), channel_id=1, source_target_pairs={{4,0},{8,4},{12,8},{16,12},{20,16},{24,20},{28,24},{32,28},{36,32}... | collective-permute-start | bytes 786440 | tf_op jit(solution)/shard_map/ppermute | solution.py:14
  186.7 2.0 %collective-permute-done.9 = bf16[2,128,512]{2,1,0:T(8,128)(2,1)} collective-permute-done((bf16[2,128,512]{2,1,0:T(8,128)(2,1)}, bf16[2,128,512]{2,1,0:T(8,128)(2,1)}, u32[]{:S(2)}, u32[]{:S(2)}) %collective-permute-start.9) | collective-permute-done | bytes 262176 | tf_op jit(solution)/shard_map/ppermute | solution.py:14
  (111 shorter events, 28.9 us)
Async XLA Ops:
  7.2 39.8 %copy-start = (bf16[512,2048]{1,0:T(8,128)(2,1)S(1)}, bf16[512,2048]{1,0:T(8,128)(2,1)}, u32[]{:S(2)}) copy-start(bf16[512,2048]{1,0:T(8,128)(2,1)} %param.11) | copy-start | bytes 6291460
  7.2 82.0 %reduce-scatter.2.cloned.1.call-start = ((), (), s32[]{:S(2)}) async-start(), calls=%async_computation.2 | async-start | bytes 655360 | tf_op jit(solution)/shard_map/reduce_scatter | solution.py:84
  9.5 19.3 %collective-permute-start = (bf16[2,128,512]{1,2,0:T(8,128)(2,1)S(1)}, bf16[2,128,512]{1,2,0:T(8,128)(2,1)S(1)}, u32[]{:S(2)}, u32[]{:S(2)}) collective-permute-start(bf16[2,128,512]{1,2,0:T(8,128)(2,1)S(1)} %pad_maximum_fusion.1), channel_id=1, source_target_pairs={{0,4},{4,8},{8,12},{12,16},{16,20},{20,24},{24,28},{28,32},{32,36}... | collective-permute-start | bytes 786440 | tf_op jit(solution)/shard_map/ppermute | solution.py:14
  13.7 18.0 %collective-permute-start.2 = (bf16[2,128,512]{1,2,0:T(8,128)(2,1)S(1)}, bf16[2,128,512]{1,2,0:T(8,128)(2,1)S(1)}, u32[]{:S(2)}, u32[]{:S(2)}) collective-permute-start(bf16[2,128,512]{1,2,0:T(8,128)(2,1)S(1)} %pad_maximum_fusion.1), channel_id=1, source_target_pairs={{4,0},{8,4},{12,8},{16,12},{20,16},{24,20},{28,24},{32,28},{36,32}... | collective-permute-start | bytes 786440 | tf_op jit(solution)/shard_map/ppermute | solution.py:14
  28.8 13.6 %collective-permute-start.1 = (bf16[2,128,512]{1,2,0:T(8,128)(2,1)S(1)}, bf16[2,128,512]{1,2,0:T(8,128)(2,1)S(1)}, u32[]{:S(2)}, u32[]{:S(2)}) collective-permute-start(bf16[2,128,512]{1,2,0:T(8,128)(2,1)S(1)} %collective-permute-done), channel_id=1, source_target_pairs={{0,4},{4,8},{8,12},{12,16},{16,20},{20,24},{24,28},{28,32},{32,36}... | collective-permute-start | bytes 786440 | tf_op jit(solution)/shard_map/ppermute | solution.py:14
  31.8 12.9 %collective-permute-start.3 = (bf16[2,128,512]{1,2,0:T(8,128)(2,1)S(1)}, bf16[2,128,512]{1,2,0:T(8,128)(2,1)S(1)}, u32[]{:S(2)}, u32[]{:S(2)}) collective-permute-start(bf16[2,128,512]{1,2,0:T(8,128)(2,1)S(1)} %collective-permute-done.2), channel_id=1, source_target_pairs={{4,0},{8,4},{12,8},{16,12},{20,16},{24,20},{28,24},{32,28},{36,32}... | collective-permute-start | bytes 786440 | tf_op jit(solution)/shard_map/ppermute | solution.py:14
  48.2 55.1 %copy-start.14 = (bf16[128,512]{1,0:T(8,128)(2,1)S(1)}, bf16[128,512]{1,0:T(8,128)(2,1)}, u32[]{:S(2)}) copy-start(bf16[128,512]{1,0:T(8,128)(2,1)} %param.13) | copy-start | bytes 393220
  90.2 12.6 %collective-permute-start.4 = (bf16[15,512]{1,0:T(8,128)(2,1)S(1)}, bf16[15,512]{1,0:T(8,128)(2,1)S(1)}, u32[]{:S(2)}, u32[]{:S(2)}) collective-permute-start(bf16[15,512]{1,0:T(8,128)(2,1)S(1)} %get-tuple-element.27), channel_id=1, source_target_pairs={{0,4},{4,8},{8,12},{12,16},{16,20},{20,24},{24,28},{28,32},{32,36}... | collective-permute-start | bytes 46088 | tf_op jit(solution)/shard_map/ppermute | solution.py:22
  93.8 9.4 %collective-permute-start.5 = (bf16[15,512]{1,0:T(8,128)(2,1)S(1)}, bf16[15,512]{1,0:T(8,128)(2,1)S(1)}, u32[]{:S(2)}, u32[]{:S(2)}) collective-permute-start(bf16[15,512]{1,0:T(8,128)(2,1)S(1)} %get-tuple-element.28), channel_id=1, source_target_pairs={{4,0},{8,4},{12,8},{16,12},{20,16},{24,20},{28,24},{32,28},{36,32}... | collective-permute-start | bytes 46088 | tf_op jit(solution)/shard_map/ppermute | solution.py:25
  103.3 14.3 %copy-start.15 = (bf16[128,512]{1,0:T(8,128)(2,1)S(1)}, bf16[128,512]{1,0:T(8,128)(2,1)}, u32[]{:S(2)}) copy-start(bf16[128,512]{1,0:T(8,128)(2,1)} %param.13) | copy-start | bytes 393220
  103.3 14.3 %copy-start.16 = (f32[1,512]{1,0:T(1,128)S(1)}, f32[1,512]{1,0:T(1,128)}, u32[]{:S(2)}) copy-start(f32[1,512]{1,0:T(1,128)} %get-tuple-element.32) | copy-start | bytes 6148
  103.3 14.3 %copy-start.17 = (f32[1,512]{1,0:T(1,128)S(1)}, f32[1,512]{1,0:T(1,128)}, u32[]{:S(2)}) copy-start(f32[1,512]{1,0:T(1,128)} %get-tuple-element.33) | copy-start | bytes 6148
  105.8 10.4 %collective-permute-start.6 = (bf16[15,512]{1,0:T(8,128)(2,1)S(1)}, bf16[15,512]{1,0:T(8,128)(2,1)S(1)}, u32[]{:S(2)}, u32[]{:S(2)}) collective-permute-start(bf16[15,512]{1,0:T(8,128)(2,1)S(1)} %get-tuple-element.25), channel_id=1, source_target_pairs={{0,4},{4,8},{8,12},{12,16},{16,20},{20,24},{24,28},{28,32},{32,36}... | collective-permute-start | bytes 46088 | tf_op jit(solution)/shard_map/ppermute | solution.py:22
  107.7 9.9 %collective-permute-start.7 = (bf16[15,512]{1,0:T(8,128)(2,1)S(1)}, bf16[15,512]{1,0:T(8,128)(2,1)S(1)}, u32[]{:S(2)}, u32[]{:S(2)}) collective-permute-start(bf16[15,512]{1,0:T(8,128)(2,1)S(1)} %get-tuple-element.26), channel_id=1, source_target_pairs={{4,0},{8,4},{12,8},{16,12},{20,16},{24,20},{28,24},{32,28},{36,32}... | collective-permute-start | bytes 46088 | tf_op jit(solution)/shard_map/ppermute | solution.py:25
  118.6 21.8 %copy-start.13 = (bf16[128,512]{1,0:T(8,128)(2,1)}, bf16[128,512]{1,0:T(8,128)(2,1)S(1)}, u32[]{:S(2)}) copy-start(bf16[128,512]{1,0:T(8,128)(2,1)S(1)} %fusion.44) | copy-start | bytes 393220
  153.8 19.5 %copy-start.1 = (f32[1,640,512]{2,1,0:T(8,128)S(1)}, f32[1,640,512]{2,1,0:T(8,128)}, u32[]{:S(2)}) copy-start(f32[1,640,512]{2,1,0:T(8,128)} %copy.41) | copy-start | bytes 3932164
  155.5 16.5 %collective-permute-start.8 = (bf16[2,128,512]{2,1,0:T(8,128)(2,1)S(1)}, bf16[2,128,512]{2,1,0:T(8,128)(2,1)S(1)}, u32[]{:S(2)}, u32[]{:S(2)}) collective-permute-start(bf16[2,128,512]{2,1,0:T(8,128)(2,1)S(1)} %get-tuple-element.19), channel_id=1, source_target_pairs={{0,4},{4,8},{8,12},{12,16},{16,20},{20,24},{24,28},{28,32},{32,36}... | collective-permute-start | bytes 786440 | tf_op jit(solution)/shard_map/ppermute | solution.py:14
  157.4 27.4 %copy-start.8 = (bf16[128,512]{1,0:T(8,128)(2,1)S(1)}, bf16[128,512]{1,0:T(8,128)(2,1)}, u32[]{:S(2)}) copy-start(bf16[128,512]{1,0:T(8,128)(2,1)} %copy-done.7) | copy-start | bytes 393220
  157.4 27.4 %copy-start.12 = (f32[128,512]{1,0:T(8,128)S(1)}, f32[128,512]{1,0:T(8,128)}, u32[]{:S(2)}) copy-start(f32[128,512]{1,0:T(8,128)} %get-tuple-element.16) | copy-start | bytes 786436
  157.4 28.2 %copy-start.3 = (bf16[1,640,512]{1,2,0:T(8,128)(2,1)S(1)}, bf16[1,640,512]{1,2,0:T(8,128)(2,1)}, u32[]{:S(2)}) copy-start(bf16[1,640,512]{1,2,0:T(8,128)(2,1)} %copy-done.2) | copy-start | bytes 1966084
  157.4 28.2 %copy-start.6 = (bf16[4,128,640]{1,2,0:T(8,128)(2,1)S(1)}, bf16[4,128,640]{1,2,0:T(8,128)(2,1)}, u32[]{:S(2)}) copy-start(bf16[4,128,640]{1,2,0:T(8,128)(2,1)} %fusion.5) | copy-start | bytes 1966084
  157.5 15.9 %collective-permute-start.10 = (bf16[2,128,512]{2,1,0:T(8,128)(2,1)S(1)}, bf16[2,128,512]{2,1,0:T(8,128)(2,1)S(1)}, u32[]{:S(2)}, u32[]{:S(2)}) collective-permute-start(bf16[2,128,512]{2,1,0:T(8,128)(2,1)S(1)} %get-tuple-element.20), channel_id=1, source_target_pairs={{4,0},{8,4},{12,8},{16,12},{20,16},{24,20},{28,24},{32,28},{36,32}... | collective-permute-start | bytes 786440 | tf_op jit(solution)/shard_map/ppermute | solution.py:14
  174.3 14.4 %collective-permute-start.9 = (bf16[2,128,512]{2,1,0:T(8,128)(2,1)}, bf16[2,128,512]{2,1,0:T(8,128)(2,1)}, u32[]{:S(2)}, u32[]{:S(2)}) collective-permute-start(bf16[2,128,512]{2,1,0:T(8,128)(2,1)} %get-tuple-element.17), channel_id=1, source_target_pairs={{0,4},{4,8},{8,12},{12,16},{16,20},{20,24},{24,28},{28,32},{32,36}... | collective-permute-start | bytes 786440 | tf_op jit(solution)/shard_map/ppermute | solution.py:14
  176.2 13.7 %collective-permute-start.11 = (bf16[2,128,512]{2,1,0:T(8,128)(2,1)}, bf16[2,128,512]{2,1,0:T(8,128)(2,1)}, u32[]{:S(2)}, u32[]{:S(2)}) collective-permute-start(bf16[2,128,512]{2,1,0:T(8,128)(2,1)} %get-tuple-element.18), channel_id=1, source_target_pairs={{4,0},{8,4},{12,8},{16,12},{20,16},{24,20},{28,24},{32,28},{36,32}... | collective-permute-start | bytes 786440 | tf_op jit(solution)/shard_map/ppermute | solution.py:14
  (21 other events, 231.9 us)
Sparse Core Ops, SparseCore 0:
  48.3 40.8 reduce-scatter.1
